TPU v7x, 128 devices: a whole 4x4x4 slice. The times are simulated.
128 devices in a mesh: row: 16 (over y, z_lo, core), col: 8 (over x, z_hi).
Axes of the slice: x: 4, y: 4, z: 4 (z_hi: 2, z_lo: 2; z = z_hi * 2 + z_lo), core: 2. Of those that a mesh axis runs over, the one named last changes fastest.
Arguments:
- pair: bfloat16 [768, 768, 128], P('row', 'col'), may hold values from -6 to 6
- bins: int32 [768, 768], P('row', 'col'), may hold values from 0 to 14
- mask: int32 [768], replicated, may hold values 0 or 1
- emb_table: bfloat16 [15, 128], replicated, may hold values from -6 to 6
- ln_gain: float32 [128], replicated, may hold values from 0.1 to 1.9
- ln_bias: float32 [128], replicated, may hold values from -3 to 3
- proj_weight: bfloat16 [128, 512], replicated, may hold values from -0.5 to 0.5
- gate_weight: bfloat16 [128, 128], replicated, may hold values from -0.5 to 0.5
- norm_gain: float32 [128], replicated, may hold values from 0.1 to 1.9
- norm_bias: float32 [128], replicated, may hold values from -3 to 3
- out_weight: bfloat16 [128, 128], replicated, may hold values from -0.5 to 0.5
Outputs:
- pair_out: bfloat16 [768, 768, 128], P('row', 'col')
All inputs are finite; a program needn't handle non-finite values.
Results may differ from a plain program's by a relative error of at most 0.0085.
Values may be sent and summed in bfloat16 or wider, within the bound.
No kernel may reach another device: no remote copies, remote signals or barrier semaphores. Data moves between devices by JAX's collectives and lax.ppermute only.
A program may use at most 128 MiB of HBM per device.

v0:
```python
import jax
import jax.numpy as jnp
from jax import lax
from jax.sharding import PartitionSpec as P


def layer_norm(values, gain, bias):
    mean = jnp.mean(values, axis=-1, keepdims=True)
    centred = values - mean
    var = jnp.mean(centred * centred, axis=-1, keepdims=True)
    return centred / jnp.sqrt(var + 1e-05) * gain + bias


def body(
    pair,
    bins,
    mask,
    emb_table,
    ln_gain,
    ln_bias,
    proj_weight,
    gate_weight,
    norm_gain,
    norm_bias,
    out_weight,
):
    rows = pair.shape[0]
    cols = pair.shape[1]
    hidden = proj_weight.shape[1] // 4
    row_start = lax.axis_index("row") * rows
    col_start = lax.axis_index("col") * cols
    mask_f = mask.astype(jnp.float32)
    mask_rows = lax.dynamic_slice_in_dim(mask_f, row_start, rows)
    mask_cols = lax.dynamic_slice_in_dim(mask_f, col_start, cols)
    levels = jnp.arange(emb_table.shape[0], dtype=jnp.int32)
    one_hot = (bins[:, :, None] == levels[None, None, :]).astype(jnp.bfloat16)
    embedded = jnp.einsum("ijb,bc->ijc", one_hot, emb_table, preferred_element_type=jnp.float32)
    summed = pair.astype(jnp.float32) + embedded
    normed = layer_norm(summed, ln_gain, ln_bias).astype(jnp.bfloat16)
    proj = jnp.dot(normed, proj_weight, preferred_element_type=jnp.float32)
    pair_mask = mask_rows[:, None, None] * mask_cols[None, :, None]
    left = (
        pair_mask * jax.nn.sigmoid(proj[..., hidden : 2 * hidden]) * proj[..., 0:hidden]
    ).astype(jnp.bfloat16)
    right = (
        pair_mask
        * jax.nn.sigmoid(proj[..., 3 * hidden : 4 * hidden])
        * proj[..., 2 * hidden : 3 * hidden]
    ).astype(jnp.bfloat16)
    gate = jax.nn.sigmoid(jnp.dot(normed, gate_weight, preferred_element_type=jnp.float32))
    partial_tri = jnp.einsum(
        "ikc,jkc->ijc",
        left,
        lax.all_gather(right, "row", axis=0, tiled=True),
        preferred_element_type=jnp.float32,
    )
    tri = lax.psum_scatter(
        partial_tri.astype(jnp.bfloat16), "col", scatter_dimension=1, tiled=True
    ).astype(jnp.float32)
    tri_normed = layer_norm(tri, norm_gain, norm_bias).astype(jnp.bfloat16)
    update = gate * jnp.dot(tri_normed, out_weight, preferred_element_type=jnp.float32)
    return (summed + update).astype(jnp.bfloat16)


def solution(mesh):
    placed = (P("row", "col", None), P("row", "col"), P(), P(), P(), P(), P(), P(), P(), P(), P())
    return jax.shard_map(
        body, mesh=mesh, in_specs=placed, out_specs=P("row", "col", None), check_vma=False
    )
```

profile of v0, /device:TPU:1, one launch (start us, length us, event | category | flops | bytes accessed | tf_op | source)
XLA Modules:
  0.0 327.6 jit_solution(3876764700117303242)
XLA Ops:
  6.5 0.0 copy-start
  6.5 0.0 all-gather.2.cloned.1.call-start
  6.5 0.7 convert_element_type.33
  7.3 0.1 dynamic_slice.6
  7.3 0.1 dynamic_slice.7
  7.4 0.0 copy-start.5
  7.4 0.0 copy-start.6
  7.4 2.8 fusion.24
  10.3 1.6 multiply_reduce_fusion
  11.9 0.1 broadcast_multiply_fusion
  12.0 0.0 copy-done.5
  12.0 0.0 copy-done.6
  12.0 1.6 add_convert_fusion.1
  13.7 0.0 copy-start.2
  13.7 1.0 copy-done.2
  14.7 0.0 copy-done
  14.7 1.4 fusion.18
  16.0 2.4 fusion.6
  18.5 0.0 all-gather.2.cloned.1.call-update
  18.5 0.0 reduce-scatter.2.cloned.1.call-start
  18.6 2.7 copy.28
  21.3 102.5 %all-gather.2.cloned.1.call-done = bf16[768,96,128]{2,1,0:T(8,128)(2,1)} async-done(((bf16[48,96,128]{2,1,0:T(8,128)(2,1)}), bf16[768,96,128]{2,1,0:T(8,128)(2,1)}) %all-gather.2.cloned.1.call-update) | async-done | bytes 18874384 | tf_op jit(solution)/shard_map/all_gather | solution.py:54
  123.8 29.6 %copy.27 = bf16[768,96,128]{1,0,2:T(8,128)(2,1)} copy(bf16[768,96,128]{2,1,0:T(8,128)(2,1)} %all-gather.2.cloned.1.call-done) | data formatting | bytes 37748736 | tf_op jit(solution)/shard_map/all_gather | solution.py:54
  153.4 17.2 %convert_bitcast_fusion = bf16[48,768,128]{1,0,2:T(8,128)(2,1)} fusion(bf16[768,96,128]{1,0,2:T(8,128)(2,1)} %copy.27, bf16[48,96,128]{1,0,2:T(8,128)(2,1)} %copy.28), kind=kOutput, calls=%fused_computation | convolution fusion | flops 910688256 | bytes 29491200 | tf_op jit(solution)/shard_map/ikc,jkc->ijc/dot_general | solution.py:51
  170.6 14.1 %copy.29 = bf16[48,768,128]{2,0,1:T(8,128)(2,1)} copy(bf16[48,768,128]{1,0,2:T(8,128)(2,1)} %convert_bitcast_fusion) | data formatting | bytes 18874368 | tf_op jit(solution)/shard_map/convert_element_type | solution.py:58
  184.7 0.0 copy-start.4
  184.7 0.0 reduce-scatter.2.cloned.1.call-update
  184.7 0.7 copy-done.4
  185.5 0.0 copy-start.7
  185.5 0.0 copy-start.8
  185.5 3.1 fusion.21
  188.6 122.2 %reduce-scatter.2.cloned.1.call-done = bf16[48,96,128]{2,0,1:T(8,128)(2,1)} async-done(((bf16[48,768,128]{2,0,1:T(8,128)(2,1)}), bf16[48,96,128]{2,0,1:T(8,128)(2,1)}) %reduce-scatter.2.cloned.1.call-update) | async-done | bytes 1179664 | tf_op jit(solution)/shard_map/reduce_scatter | solution.py:57
  310.9 2.0 convert_reduce_fusion
  312.8 0.0 copy-start.9
  312.8 0.1 copy.30
  312.9 0.1 copy.31
  313.0 2.5 fusion.2
  315.5 0.1 copy.32
  315.6 0.1 copy.33
  315.7 0.0 copy-done.7
  315.7 0.0 copy-done.8
  315.7 0.0 copy-start.3
  315.7 3.1 fusion.5
  318.8 0.0 copy-done.9
  318.8 0.0 copy-done.3
  318.9 0.0 copy-start.1
  318.9 1.9 add_convert_fusion
  320.8 0.0 copy-done.1
  (4 shorter events, 0.1 us)
Async XLA Ops:
  6.5 8.1 %copy-start = (bf16[128,512]{1,0:T(8,128)(2,1)S(1)}, bf16[128,512]{1,0:T(8,128)(2,1)}, u32[]{:S(2)}) copy-start(bf16[128,512]{1,0:T(8,128)(2,1)} %param.17) | copy-start | bytes 393220
  6.5 117.3 %all-gather.2.cloned.1.call-start = ((), (), s32[]{:S(2)}) async-start(), calls=%async_computation.1 | async-start | bytes 20054016 | tf_op jit(solution)/shard_map/all_gather | solution.py:54
  7.4 4.6 %copy-start.5 = (f32[128]{0:T(128)S(1)}, f32[128]{0:T(128)}, u32[]{:S(2)}) copy-start(f32[128]{0:T(128)} %param.16) | copy-start | bytes 1540
  7.4 4.6 %copy-start.6 = (f32[128]{0:T(128)S(1)}, f32[128]{0:T(128)}, u32[]{:S(2)}) copy-start(f32[128]{0:T(128)} %param.15) | copy-start | bytes 1540
  13.7 1.0 copy-start.2
  18.5 292.3 %reduce-scatter.2.cloned.1.call-start = ((), (), s32[]{:S(2)}) async-start(), calls=%async_computation.2 | async-start | bytes 10616832 | tf_op jit(solution)/shard_map/reduce_scatter | solution.py:57
  184.7 0.8 copy-start.4
  185.5 130.2 %copy-start.7 = (f32[128]{0:T(128)S(1)}, f32[128]{0:T(128)}, u32[]{:S(2)}) copy-start(f32[128]{0:T(128)} %param.20) | copy-start | bytes 1540
  185.5 130.2 %copy-start.8 = (f32[128]{0:T(128)S(1)}, f32[128]{0:T(128)}, u32[]{:S(2)}) copy-start(f32[128]{0:T(128)} %param.19) | copy-start | bytes 1540
  312.8 6.0 %copy-start.9 = (bf16[128,128]{1,0:T(8,128)(2,1)S(1)}, bf16[128,128]{1,0:T(8,128)(2,1)}, u32[]{:S(2)}) copy-start(bf16[128,128]{1,0:T(8,128)(2,1)} %param.21) | copy-start | bytes 98308
  315.7 3.2 copy-start.3
  318.9 1.9 copy-start.1
Sparse Core Ops, SparseCore 0:
  18.6 105.1 all-gather.1
  184.8 125.9 reduce-scatter.1
where the time goes:
time: 329 us; the launch traced here: 328 us
  waiting for transfers between devices  225 us (68%)
  local copies, waits for them, and re-layouts  48.6 us (15%)
  matrix products  26.5 us (8%)
  other arithmetic  14.1 us (4%)
  between operations  13.6 us (4%)
    reduce_scatter x1, waiting for transfers between devices, body(): lax.psum_scatter(partial_tri.astype(jnp.bfloat16), 'col', scatter_dimensi...  122 us
    all_gather x1, waiting for transfers between devices, body(): lax.all_gather(right, 'row', axis=0, tiled=True)  103 us
    all_gather x1, local copies, waits for them, and re-layouts, body(): lax.all_gather(right, 'row', axis=0, tiled=True)  29.6 us
    dot_general x1, matrix products, body(): jnp.einsum('ikc,jkc->ijc', left, lax.all_gather(right, 'row', axis=0, til...  17.2 us
    convert_element_type x1, local copies, waits for them, and re-layouts, body(): partial_tri.astype(jnp.bfloat16)  14.1 us
  transfers between devices with their start and end apart: 2, of which 2 were waited for; matrix products, arithmetic and copies ran while one was open for 2% of the time, Pallas kernels for 0%

commit v1 on v0

v1 whole, which is shorter than its diff:
```python
import jax
import jax.numpy as jnp
from jax import lax
from jax.experimental import pallas as pl
from jax.experimental.pallas import tpu as pltpu
from jax.sharding import PartitionSpec as P

EPS = 1e-5
F32 = jnp.float32
BF16 = jnp.bfloat16
NT = (((1,), (1,)), ((), ()))
NN = (((1,), (0,)), ((), ()))
VMEM = 48 * 1024 * 1024


def column_rows(col):
    if col < 8:
        return [8 * b + col for b in range(4)]
    p = col - 8
    return [32 + p, 40 + p, 36 + p, 44 + p]


def sigmoid(x):
    return 0.5 * jnp.tanh(0.5 * x) + 0.5


def norm_sublanes(x, gain, bias):
    mean = jnp.mean(x, axis=0, keepdims=True)
    centred = x - mean
    var = jnp.mean(centred * centred, axis=0, keepdims=True)
    return (centred * lax.rsqrt(var + EPS) * gain + bias).astype(BF16)


def dot(a, b, dims=NN):
    return lax.dot_general(a, b, dims, preferred_element_type=F32)


def one_hot_rows(code):
    level = lax.broadcasted_iota(jnp.int32, (16, code.shape[1]), 0)
    return jnp.where((code & 15) == level, 1.0, 0.0).astype(BF16)


def project_kernel(pair, code, eye, emb_t, gain, bias, weight_t, out, normed_out):
    low = lax.broadcasted_iota(jnp.int32, (128, 128), 1) < 64
    for half in range(2):
        gs = [2 * half, 2 * half + 1, 2 * half + 4, 2 * half + 5]
        ps = [2 * half, 2 * half + 1]
        cols = gs + [8 + p for p in ps]
        rows = [pair[i] for c in cols for i in column_rows(c)]
        x = jnp.concatenate(rows, axis=0)
        codes = jnp.concatenate([code[0, c : c + 1, :] for c in cols], axis=1)
        summed = dot(eye[...], x, NT) + dot(emb_t[...], one_hot_rows(codes))
        normed = norm_sublanes(summed, gain[...], bias[...])
        for n, c in enumerate(cols):
            normed_out[0, c] = normed[:, 128 * n : 128 * (n + 1)]
        proj = dot(weight_t[...], normed)
        keep = jnp.where(codes >= 16, 1.0, 0.0)
        left = keep * sigmoid(proj[128:256]) * proj[0:128]
        right = keep * sigmoid(proj[384:512]) * proj[256:384]
        for n, g in enumerate(gs):
            p = 4 + n % 2
            lane = slice(128 * n, 128 * (n + 1))
            tail = slice(128 * p, 128 * (p + 1))
            left_tail, right_tail = left[:, tail], right[:, tail]
            if g < 4:
                left_tail = pltpu.roll(left_tail, 64, 1)
            else:
                right_tail = pltpu.roll(right_tail, 64, 1)
            out[g] = left[:, lane].astype(BF16)
            out[8 + g] = jnp.where(low, right[:, lane], left_tail).astype(BF16)
            out[16 + g] = jnp.where(low, right_tail, right[:, lane]).astype(BF16)


def project(pair, code, eye, emb_t, gain, bias, weight_t):
    whole = lambda a: pl.BlockSpec(a.shape, lambda m: (0,) * a.ndim)
    return pl.pallas_call(
        project_kernel,
        grid=(3,),
        in_specs=[
            pl.BlockSpec((48, 32, 128), lambda m: (0, m, 0)),
            pl.BlockSpec((1, 12, 128), lambda m: (m, 0, 0)),
            whole(eye),
            whole(emb_t),
            whole(gain),
            whole(bias),
            whole(weight_t),
        ],
        out_specs=[
            pl.BlockSpec((24, 128, 128), lambda m: (m, 0, 0)),
            pl.BlockSpec((1, 12, 128, 128), lambda m: (m, 0, 0, 0)),
        ],
        out_shape=[
            jax.ShapeDtypeStruct((72, 128, 128), BF16),
            jax.ShapeDtypeStruct((3, 12, 128, 128), BF16),
        ],
        compiler_params=pltpu.CompilerParams(vmem_limit_bytes=VMEM),
    )(pair, code, eye, emb_t, gain, bias, weight_t)


LEFT_AT = [(0, 0), (0, 1), (0, 2), (0, 3), (1, 2), (1, 3)]
RIGHT_AT = [(1, 0), (1, 1), (2, 2), (2, 3), (2, 0), (2, 1)]


def roll_slots(x, by):
    by %= 4
    return x if by == 0 else pltpu.roll(x, 32 * by, 1)


def triangle_kernel(recv, out, left, right, tri):
    slot = lax.broadcasted_iota(jnp.int32, (8, 128), 1) // 32

    def pick(parts):
        got = parts[0]
        for z in range(1, 4):
            got = jnp.where(slot == z, parts[z], got)
        return got

    def gather(r, _):
        base = pl.multiple_of(48 * r, 16)
        for tile in range(6):
            src = {}
            for z in range(4):
                q, m = divmod(4 * tile + z, 3)
                block = recv[8 * r + q, 24 * m : 24 * (m + 1), :].astype(F32)
                for h in range(3):
                    src[z, h] = block[8 * h : 8 * (h + 1)]
            for at, dest in ((LEFT_AT, left), (RIGHT_AT, right)):
                got = [pick([roll_slots(src[z, h], z - s) for z in range(4)]) for h, s in at]
                for b in range(0, 6, 2):
                    dest[pl.ds(base + 8 * b, 16), 128 * tile : 128 * (tile + 1)] = (
                        jnp.concatenate(got[b : b + 2], axis=0).astype(BF16)
                    )
        return 0

    lax.fori_loop(0, 16, gather, 0)
    for block in range(3):
        rows = slice(256 * block, 256 * (block + 1))
        tri[rows, :] = dot(left[rows, :], right[...], NT)

    def scatter(r, _):
        base = pl.multiple_of(48 * r, 16)
        for q in range(8):
            full, tails = [], []
            for m in range(3):
                tile, z = divmod(3 * q + m, 4)
                cols = slice(128 * tile, 128 * (tile + 1))
                piece = [tri[pl.ds(base + 8 * b, 8), cols] for b in range(6)]
                full.append(pick([roll_slots(piece[b], b - z) for b in range(4)]))
                tail = pick(
                    [roll_slots(piece[4 + s % 2], s - z) for s in range(4)]
                )
                tails.append(jnp.where(slot[:4] < 2, tail[:4], tail[4:]))
            out[8 * r + q] = jnp.concatenate(full + tails, axis=0).astype(BF16)
        return 0

    lax.fori_loop(0, 16, scatter, 0)


def triangle(recv):
    return pl.pallas_call(
        triangle_kernel,
        in_specs=[pl.BlockSpec(memory_space=pltpu.VMEM)],
        out_specs=pl.BlockSpec(memory_space=pltpu.VMEM),
        out_shape=jax.ShapeDtypeStruct((128, 36, 128), BF16),
        scratch_shapes=[
            pltpu.VMEM((768, 768), BF16),
            pltpu.VMEM((768, 768), BF16),
            pltpu.VMEM((768, 768), F32),
        ],
        compiler_params=pltpu.CompilerParams(vmem_limit_bytes=VMEM),
    )(recv)


def update_kernel(
    tri, tri_tail, normed, pair, code, eye, emb, gain, bias, gate_weight, out_weight, out
):
    for col in range(12):
        sums = (tri[col] if col < 8 else tri_tail[col - 8]).astype(F32)
        tri_normed = norm_sublanes(sums, gain[...], bias[...])
        hot = one_hot_rows(code[0, col : col + 1, :])
        turned = dot(eye[...], jnp.concatenate([tri_normed, normed[0, col], hot], axis=0), NT)
        turned = turned.astype(BF16)
        update = dot(turned[:, :128], out_weight[...])
        gate = sigmoid(dot(turned[:, 128:256], gate_weight[...]))
        embedded = dot(turned[:, 256:], emb[...])
        rows = column_rows(col)
        x = jnp.concatenate([pair[i] for i in rows], axis=0).astype(F32)
        result = (x + embedded + gate * update).astype(BF16)
        for s, i in enumerate(rows):
            out[i] = result[32 * s : 32 * (s + 1)]


def update(tri, normed, pair, code, eye, emb, gain, bias, gate_weight, out_weight):
    whole = lambda a: pl.BlockSpec(a.shape, lambda m: (0,) * a.ndim)
    return pl.pallas_call(
        update_kernel,
        grid=(3,),
        in_specs=[
            pl.BlockSpec((8, 128, 128), lambda m: (m, 0, 0)),
            pl.BlockSpec((4, 128, 128), lambda m: (6 + m, 0, 0)),
            pl.BlockSpec((1, 12, 128, 128), lambda m: (m, 0, 0, 0)),
            pl.BlockSpec((48, 32, 128), lambda m: (0, m, 0)),
            pl.BlockSpec((1, 12, 128), lambda m: (m, 0, 0)),
            whole(eye),
            whole(emb),
            whole(gain),
            whole(bias),
            whole(gate_weight),
            whole(out_weight),
        ],
        out_specs=pl.BlockSpec((48, 32, 128), lambda m: (0, m, 0)),
        out_shape=jax.ShapeDtypeStruct((48, 96, 128), BF16),
        compiler_params=pltpu.CompilerParams(vmem_limit_bytes=VMEM),
    )(tri, tri, normed, pair, code, eye, emb, gain, bias, gate_weight, out_weight)


def pair_codes(bins, mask):
    rows, cols = bins.shape
    mask_rows = lax.dynamic_slice_in_dim(mask, lax.axis_index("row") * rows, rows)
    mask_cols = lax.dynamic_slice_in_dim(mask, lax.axis_index("col") * cols, cols)
    code = bins + 16 * mask_rows[:, None] * mask_cols[None, :]
    code = code.reshape(6, 8, 3, 32)
    head = code[:4].transpose(2, 1, 0, 3).reshape(3, 8, 128)
    tail = code[4:].reshape(2, 2, 4, 3, 32).transpose(3, 2, 1, 0, 4).reshape(3, 4, 128)
    return jnp.concatenate([head, tail], axis=1)


def body(
    pair,
    bins,
    mask,
    emb_table,
    ln_gain,
    ln_bias,
    proj_weight,
    gate_weight,
    norm_gain,
    norm_bias,
    out_weight,
):
    code = pair_codes(bins, mask)
    eye = jnp.eye(128, dtype=BF16)
    emb = jnp.pad(emb_table, ((0, 1), (0, 0)))
    column = lambda v: v.reshape(128, 1)
    sides, normed = project(
        pair, code, eye, emb.T, column(ln_gain), column(ln_bias), proj_weight.T
    )
    recv = lax.all_to_all(sides.transpose(1, 0, 2), ("row", "col"), 0, 0, tiled=True)
    sums = lax.all_to_all(triangle(recv), ("row", "col"), 0, 0, tiled=True)
    return update(
        sums.transpose(1, 0, 2),
        normed,
        pair,
        code,
        eye,
        emb,
        column(norm_gain),
        column(norm_bias),
        gate_weight,
        out_weight,
    )


def solution(mesh):
    placed = (P("row", "col", None), P("row", "col"), P(), P(), P(), P(), P(), P(), P(), P(), P())
    return jax.shard_map(
        body, mesh=mesh, in_specs=placed, out_specs=P("row", "col", None), check_vma=False
    )
```

time: 329 us -> 102 us (0.31)
  waiting for transfers between devices: 225 us -> 21.7 us
  blocking collectives: 0 us -> 44.7 us
  local copies, waits for them, and re-layouts: 48.6 us -> 9.18 us
  matrix products: 26.5 us -> 0 us
  Pallas kernels: 0 us -> 19.3 us
  between operations: 13.6 us -> 0.14 us
  other arithmetic: 14.1 us -> 1.58 us
  starting transfers between devices: 0.04 us -> 4.76 us
    reduce_scatter x1 -> x0, waiting for transfers between devices: 122 us -> none  [body(): lax.psum_scatter(partial_tri.astype(jnp.bfloat16), 'col', scatter_dimensi...]
    all_gather x1 -> x0, waiting for transfers between devices: 103 us -> none  [body(): lax.all_gather(right, 'row', axis=0, tiled=True)]
    all_to_all x0 -> x1, blocking collectives: none -> 44.7 us  [body(): lax.all_to_all(sides.transpose(1, 0, 2), ('row', 'col'), 0, 0, tiled=True)]
    all_gather x1 -> x0, local copies, waits for them, and re-layouts: 29.6 us -> none  [body(): lax.all_gather(right, 'row', axis=0, tiled=True)]
    dot_general x5 -> x0, matrix products: 26.5 us -> none  [the longest x1 17.2 us: body(): jnp.einsum('ikc,jkc->ijc', left, lax.all_gather(right, 'row', axis=0, til...]
    all_to_all x0 -> x1, waiting for transfers between devices: none -> 21.7 us  [body(): sums = lax.all_to_all(triangle(recv), ('row', 'col'), 0, 0, tiled=True)]
    pallas_call x0 -> x3, Pallas kernels: none -> 19.3 us  [the longest x1 7.85 us: update(): pl.pallas_call(update_kernel, grid=(3,), in_specs=[pl.BlockSpec((8, 128,...]
    convert_element_type x2 -> x0, local copies, waits for them, and re-layouts: 16.8 us -> none  [the longest x1 14.1 us: body(): partial_tri.astype(jnp.bfloat16)]
  transfers between devices with their start and end apart: 2 -> 1, of which waited for: 2 -> 1; matrix products, arithmetic and copies ran while one was open for 2% -> 0% of each run, Pallas kernels for 0% -> 0%
where the time goes in v1:
time: 102 us; the launch traced here: 101 us
  blocking collectives  44.7 us (44%)
  waiting for transfers between devices  21.7 us (21%)
  Pallas kernels  19.3 us (19%)
  local copies, waits for them, and re-layouts  9.18 us (9%)
  starting transfers between devices  4.76 us (5%)
  other arithmetic  1.58 us (2%)
    all_to_all x1, blocking collectives, body(): lax.all_to_all(sides.transpose(1, 0, 2), ('row', 'col'), 0, 0, tiled=True)  44.7 us
    all_to_all x1, waiting for transfers between devices, body(): sums = lax.all_to_all(triangle(recv), ('row', 'col'), 0, 0, tiled=True)  21.7 us
    pallas_call x1, Pallas kernels, update(): pl.pallas_call(update_kernel, grid=(3,), in_specs=[pl.BlockSpec((8, 128,...  7.85 us
    pallas_call x1, Pallas kernels, triangle(): pl.pallas_call(triangle_kernel, in_specs=[pl.BlockSpec(memory_space=pltpu...  7.44 us
    all_to_all x1, starting transfers between devices, body(): sums = lax.all_to_all(triangle(recv), ('row', 'col'), 0, 0, tiled=True)  4.76 us
    pallas_call x1, Pallas kernels, project(): pl.pallas_call(project_kernel, grid=(3,), in_specs=[pl.BlockSpec((48, 32,...  3.99 us
    unnamed x14, local copies, waits for them, and re-layouts  2.32 us
  transfers between devices with their start and end apart: 1, of which 1 were waited for; matrix products, arithmetic and copies ran while one was open for 0% of the time, Pallas kernels for 0%

profile of v1, /device:TPU:1, one launch (start us, length us, event | category | flops | bytes accessed | tf_op | source)
XLA Modules:
  0.0 101.4 jit_solution(12991506786306059665)
XLA Ops:
  0.0 0.8 dynamic-slice_multiply_fusion
  0.8 0.8 dynamic_slice.7
  1.5 0.8 multiply_add_fusion
  2.4 0.1 slice.11
  2.5 0.1 reshape.28
  2.6 0.1 reshape.29
  2.7 0.1 reshape.30
  2.8 0.7 fusion.1
  3.5 0.1 copy.35.emb_t
  3.6 1.0 %copy.34 = bf16[128,512]{0,1:T(8,128)(2,1)S(1)} copy(bf16[128,512]{1,0:T(8,128)(2,1)} %param.17) | data formatting | bytes 262144 | tf_op args[6]
  4.6 0.8 copy.36.gain
  5.4 0.8 copy.37.bias
  6.2 0.0 copy-start
  6.2 1.3 %copy-done = bf16[48,96,128]{2,1,0:T(8,128)(2,1)S(1)} copy-done((bf16[48,96,128]{2,1,0:T(8,128)(2,1)S(1)}, bf16[48,96,128]{2,1,0:T(8,128)(2,1)}, u32[]{:S(2)}) %copy-start) | copy-done | bytes 1179672
  7.5 4.0 %shard_map.109 = (bf16[72,128,128]{2,1,0:T(8,128)(2,1)S(1)}, bf16[3,12,128,128]{3,2,1,0:T(8,128)(2,1)S(1)}) custom-call(bf16[48,96,128]{2,1,0:T(8,128)(2,1)S(1)} %copy-done, s32[3,12,128]{2,1,0:T(8,128)S(1)} %constant_dynamic-update-slice_fusion.code, bf16[128,128]{1,0:T(8,128)(2,1)S(1)} %fusion.eye, bf16[128,16]{1,0:T(8,128)(2,1)S(1)} %copy.35.emb_t, ...), custom_call_target="tpu_custom_call" | custom-call | tf_op jit(solution)/shard_map/pallas_call | solution.py:76
  11.4 1.5 %copy.44 = bf16[72,128,128]{2,0,1:T(8,128)(2,1)S(1)} copy(bf16[72,128,128]{2,1,0:T(8,128)(2,1)S(1)} %get-tuple-element.7) | data formatting | bytes 4718592 | tf_op jit(solution)/shard_map/pallas_call | solution.py:76
  13.0 44.7 %all_to_all.10.recv = bf16[128,72,128]{2,1,0:T(8,128)(2,1)S(1)} all-to-all(bf16[128,72,128]{2,1,0:T(8,128)(2,1)S(1)} %bitcast.18), channel_id=1, replica_groups=mesh['row'=16,'col'=8] {'row','col'}, dimensions={0} | all-to-all | bytes 4718592 | tf_op jit(solution)/shard_map/all_to_all | solution.py:248
  57.7 7.4 %shard_map.110 = bf16[128,36,128]{2,1,0:T(8,128)(2,1)} custom-call(bf16[128,72,128]{2,1,0:T(8,128)(2,1)S(1)} %all_to_all.10.recv), custom_call_target="tpu_custom_call" | custom-call | tf_op jit(solution)/shard_map/pallas_call | solution.py:160
  65.2 0.0 copy-start.4
  65.2 0.0 copy-start.5
  65.2 4.8 %all-to-all-start.1 = ((bf16[128,36,128]{2,1,0:T(8,128)(2,1)}), bf16[128,36,128]{2,1,0:T(8,128)(2,1)}, u32[]{:S(2)}, u32[]{:S(2)}) async-start(bf16[128,36,128]{2,1,0:T(8,128)(2,1)} %shard_map.110), calls=%async_computation.1 | async-start | bytes 2621440 | tf_op jit(solution)/shard_map/all_to_all | solution.py:249
  69.9 0.0 copy-done.4
  69.9 0.0 copy-start.1
  69.9 0.0 copy-start.2
  70.0 0.0 copy-start.3
  70.0 0.1 copy.40.gain
  70.1 0.0 copy-done.5
  70.1 0.1 copy.41.bias
  70.2 21.7 %all-to-all-done.1 = bf16[128,36,128]{2,1,0:T(8,128)(2,1)} async-done(((bf16[128,36,128]{2,1,0:T(8,128)(2,1)}), bf16[128,36,128]{2,1,0:T(8,128)(2,1)}, u32[]{:S(2)}, u32[]{:S(2)}) %all-to-all-start.1) | async-done | bytes 1179680 | tf_op jit(solution)/shard_map/all_to_all | solution.py:249
  91.9 1.6 %copy.45 = bf16[128,36,128]{2,0,1:T(8,128)(2,1)S(1)} copy(bf16[128,36,128]{2,1,0:T(8,128)(2,1)} %all-to-all-done.1) | data formatting | bytes 2359296 | tf_op jit(solution)/shard_map/all_to_all | solution.py:249
  93.5 0.0 copy-done.1
  93.5 0.0 copy-done.2
  93.5 0.0 copy-done.3
  93.5 7.9 %shard_map.111 = bf16[48,96,128]{2,1,0:T(8,128)(2,1)} custom-call(bf16[36,128,128]{2,1,0:T(8,128)(2,1)S(1)} %bitcast.15, bf16[36,128,128]{2,1,0:T(8,128)(2,1)S(1)} %bitcast.16, bf16[3,12,128,128]{3,2,1,0:T(8,128)(2,1)S(1)} %get-tuple-element.8.normed, bf16[48,96,128]{2,1,0:T(8,128)(2,1)S(1)} %copy-done.1, ...), custom_call_target="tpu_custom_call" | custom-call | tf_op jit(solution)/shard_map/pallas_call | solution.py:195
  (7 shorter events, 0.1 us)
Async XLA Ops:
  6.2 1.3 %copy-start = (bf16[48,96,128]{2,1,0:T(8,128)(2,1)S(1)}, bf16[48,96,128]{2,1,0:T(8,128)(2,1)}, u32[]{:S(2)}) copy-start(bf16[48,96,128]{2,1,0:T(8,128)(2,1)} %pair.3) | copy-start | bytes 3538948
  65.2 4.8 %copy-start.4 = (f32[128]{0:T(128)S(1)}, f32[128]{0:T(128)}, u32[]{:S(2)}) copy-start(f32[128]{0:T(128)} %param.19) | copy-start | bytes 1540
  65.2 4.9 %copy-start.5 = (f32[128]{0:T(128)S(1)}, f32[128]{0:T(128)}, u32[]{:S(2)}) copy-start(f32[128]{0:T(128)} %param.20) | copy-start | bytes 1540
  65.2 26.8 %all-to-all-start.1 = ((bf16[128,36,128]{2,1,0:T(8,128)(2,1)}), bf16[128,36,128]{2,1,0:T(8,128)(2,1)}, u32[]{:S(2)}, u32[]{:S(2)}) async-start(bf16[128,36,128]{2,1,0:T(8,128)(2,1)} %shard_map.110), calls=%async_computation.1 | async-start | bytes 2621440 | tf_op jit(solution)/shard_map/all_to_all | solution.py:249
  69.9 23.6 %copy-start.1 = (bf16[48,96,128]{2,1,0:T(8,128)(2,1)S(1)}, bf16[48,96,128]{2,1,0:T(8,128)(2,1)}, u32[]{:S(2)}) copy-start(bf16[48,96,128]{2,1,0:T(8,128)(2,1)} %pair.3) | copy-start | bytes 3538948
  69.9 23.6 %copy-start.2 = (bf16[128,128]{1,0:T(8,128)(2,1)S(1)}, bf16[128,128]{1,0:T(8,128)(2,1)}, u32[]{:S(2)}) copy-start(bf16[128,128]{1,0:T(8,128)(2,1)} %gate_weight.1) | copy-start | bytes 98308
  70.0 23.6 %copy-start.3 = (bf16[128,128]{1,0:T(8,128)(2,1)S(1)}, bf16[128,128]{1,0:T(8,128)(2,1)}, u32[]{:S(2)}) copy-start(bf16[128,128]{1,0:T(8,128)(2,1)} %out_weight.1) | copy-start | bytes 98308
